TPU v7x, 256 devices: a whole 4x4x8 slice. The times are simulated.
256 devices in a mesh: lon: 16 (over y, x_lo, core), lat: 16 (over z, x_hi).
Axes of the slice: x: 4 (x_hi: 2, x_lo: 2; x = x_hi * 2 + x_lo), y: 4, z: 8, core: 2. Of those that a mesh axis runs over, the one named last changes fastest.
Arguments:
- levels_in: bfloat16 [13, 96, 192, 512], P(None, 'lat', 'lon'), may hold values from -6 to 6
- surface: bfloat16 [96, 192, 512], P('lat', 'lon'), may hold values from -6 to 6
- latents: bfloat16 [3, 512], replicated, may hold values from -3 to 3
- level_codes: bfloat16 [13, 512], replicated, may hold values from -3 to 3
- norm_gains: float32 [6, 512], replicated, may hold values from 0.1 to 1.9
- agg_query_w: bfloat16 [512, 512], P('lat'), may hold values from -0.25 to 0.25
- agg_key_w: bfloat16 [512, 512], P('lat'), may hold values from -0.25 to 0.25
- agg_value_w: bfloat16 [512, 512], P('lat'), may hold values from -0.25 to 0.25
- agg_out_w: bfloat16 [512, 512], P('lat'), may hold values from -0.25 to 0.25
- dec_query_w: bfloat16 [512, 512], P('lat'), may hold values from -0.25 to 0.25
- dec_key_w: bfloat16 [512, 512], P('lat'), may hold values from -0.25 to 0.25
- dec_value_w: bfloat16 [512, 512], P('lat'), may hold values from -0.25 to 0.25
- dec_out_w: bfloat16 [512, 512], P('lat'), may hold values from -0.25 to 0.25
- qkv_w: bfloat16 [2, 512, 1536], P(None, 'lat'), may hold values from -0.25 to 0.25
- proj_w: bfloat16 [2, 512, 512], P(None, 'lat'), may hold values from -0.25 to 0.25
- mlp_in: bfloat16 [2, 2048, 512], P(None, 'lat'), may hold values from -0.25 to 0.25
- mlp_out: bfloat16 [2, 2048, 512], P(None, 'lat'), may hold values from -0.125 to 0.125
- regions: int32 [4, 96], P(None, 'lat'), may hold values from 0 to 2
Outputs:
- decoded: bfloat16 [13, 96, 192, 512], P(None, 'lat', 'lon')
All inputs are finite; a program needn't handle non-finite values.
Results may differ from a plain program's by a relative error of at most 0.025.
Values may be sent and summed in bfloat16 or wider, within the bound.
A program may use at most 64 MiB of HBM per device.

v0:
```python
import jax
import jax.numpy as jnp
from jax import lax
from jax.sharding import PartitionSpec as P

HEADS = 16
HD = 32
LATENT = 3
ZL = 4
WZ = 2
WLAT = 6
WLON = 12


NORM_EPSILON = 1e-05
TOP_PRECISION = lax.Precision.HIGHEST


def from_behind(block, axis, distance):
    devices = range(lax.axis_size(axis))
    route = [((i - distance) % len(devices), i) for i in devices]
    return lax.ppermute(block, axis, route)


def layer_norm(values, gain_row):
    widened = values.astype(jnp.float32)
    centre = widened - jnp.mean(widened, axis=-1, keepdims=True)
    variance = jnp.mean(centre * centre, axis=-1, keepdims=True)
    return (centre * lax.rsqrt(variance + NORM_EPSILON) * gain_row).astype(jnp.bfloat16)


def head_matrix(queries):
    query_count = queries.shape[0]
    identity = (jnp.arange(HEADS)[:, None] == jnp.arange(HEADS)[None, :]).astype(jnp.float32)
    blocked = queries.reshape(query_count, HEADS, HD)[:, :, :, None] * identity[None, :, None, :]
    return jnp.transpose(blocked, (1, 2, 0, 3)).reshape(HEADS * HD, query_count * HEADS)


def attend_levels(key_rows, value_rows, queries, level_count):
    score_scale = HD ** (-0.5)
    scores = (
        jnp.dot(
            key_rows,
            head_matrix(queries),
            precision=TOP_PRECISION,
            preferred_element_type=jnp.float32,
        )
        * score_scale
    )
    scores = scores.reshape(level_count, -1, queries.shape[0], HEADS)
    exponent = jnp.exp(scores)
    weights_bf = (exponent / jnp.sum(exponent, axis=0, keepdims=True)).astype(jnp.bfloat16)
    spread = jnp.repeat(weights_bf, HD, axis=-1).astype(jnp.float32)
    values_wide = value_rows.reshape(level_count, -1, 1, value_rows.shape[-1]).astype(jnp.float32)
    return jnp.sum(spread * values_wide, axis=0).astype(jnp.bfloat16)


def stack_queries(mixed_rows):
    points, query_count, feature_width = mixed_rows.shape
    return jnp.transpose(mixed_rows, (1, 0, 2)).reshape(query_count * points, feature_width)


def to_windows(level_grid):
    lev_count, row_count, col_count, last_size = level_grid.shape
    regrouped = level_grid.reshape(
        lev_count // WZ, WZ, row_count // WLAT, WLAT, col_count // WLON, WLON, last_size
    )
    return jnp.transpose(regrouped, (0, 2, 4, 1, 3, 5, 6)).reshape(-1, WZ * WLAT * WLON, last_size)


def from_windows(windows, lev_count, row_count, col_count):
    last_size = windows.shape[-1]
    regrouped = windows.reshape(
        lev_count // WZ, row_count // WLAT, col_count // WLON, WZ, WLAT, WLON, last_size
    )
    return jnp.transpose(regrouped, (0, 3, 1, 4, 2, 5, 6)).reshape(
        lev_count, row_count, col_count, last_size
    )


def window_ids(region_rows, col_count):
    lev_count, row_count = region_rows.shape
    id_grid = jnp.broadcast_to(region_rows[:, :, None, None], (lev_count, row_count, col_count, 1))
    return to_windows(id_grid)[:, :, 0]


def window_attention(packed, window_id):
    feature_width = packed.shape[-1] // 3
    win_count, win_size = (packed.shape[0], packed.shape[1])

    def heads_of(which_part):
        section = packed[:, :, which_part * feature_width : (which_part + 1) * feature_width]
        return section.reshape(win_count, win_size, HEADS, HD)

    scores = jnp.einsum(
        "wqhd,wkhd->whqk", heads_of(0), heads_of(1), preferred_element_type=jnp.float32
    ) * HD ** (-0.5)
    exponent = jnp.exp(scores)
    if window_id is not None:
        exponent = exponent * (window_id[:, None, :, None] == window_id[:, None, None, :]).astype(
            jnp.float32
        )
    weights_bf = (exponent / jnp.sum(exponent, axis=-1, keepdims=True)).astype(jnp.bfloat16)
    mixed_rows = jnp.einsum(
        "whqk,wkhd->wqhd", weights_bf, heads_of(2), preferred_element_type=jnp.float32
    )
    return mixed_rows.reshape(win_count, win_size, HEADS * HD).astype(jnp.bfloat16)


def fold_pair(token_rows, pieces):
    return (
        jnp.dot(token_rows, pieces[0], preferred_element_type=jnp.float32),
        jnp.dot(token_rows, pieces[1], preferred_element_type=jnp.float32),
    )


def fold_single(token_rows, weight_piece):
    return jnp.dot(token_rows, weight_piece, preferred_element_type=jnp.float32)


def hidden_terms(normed_rows, in_piece, out_piece):
    hidden = jax.nn.gelu(
        lax.dot_general(
            normed_rows, in_piece, (((1,), (1,)), ((), ())), preferred_element_type=jnp.float32
        ),
        approximate=False,
    ).astype(jnp.bfloat16)
    return jnp.dot(hidden, out_piece, preferred_element_type=jnp.float32)


def fold_hidden(normed_rows, pieces):
    return hidden_terms(normed_rows, pieces[0], pieces[1])


def roll_forward(level_grid):
    half_rows = WLAT // 2
    half_cols = WLON // 2
    turned = jnp.roll(level_grid, -1, axis=0)
    turned = jnp.concatenate(
        [turned[:, :, half_cols:], from_behind(turned[:, :, :half_cols], "lon", -1)], axis=2
    )
    return jnp.concatenate(
        [turned[:, half_rows:], from_behind(turned[:, :half_rows], "lat", -1)], axis=1
    )


def roll_back(level_grid):
    half_rows = WLAT // 2
    half_cols = WLON // 2
    row_count, col_count = (level_grid.shape[1], level_grid.shape[2])
    turned = jnp.concatenate(
        [
            from_behind(level_grid[:, row_count - half_rows :], "lat", 1),
            level_grid[:, : row_count - half_rows],
        ],
        axis=1,
    )
    return jnp.concatenate(
        [
            from_behind(turned[:, :, col_count - half_cols :], "lon", 1),
            turned[:, :, : col_count - half_cols],
        ],
        axis=2,
    )


def body(
    levels_in,
    surface,
    latents,
    level_codes,
    norm_gains,
    agg_query_w,
    agg_key_w,
    agg_value_w,
    agg_out_w,
    dec_query_w,
    dec_key_w,
    dec_value_w,
    dec_out_w,
    qkv_w,
    proj_w,
    mlp_in,
    mlp_out,
    regions,
):
    lev_count, row_count, col_count, feature_width = levels_in.shape
    point_count = row_count * col_count
    shard_rows = agg_query_w.shape[0]
    first_row = lax.axis_index("lat") * shard_rows
    latent_part = jnp.dot(
        lax.dynamic_slice_in_dim(latents, first_row, shard_rows, 1),
        agg_query_w,
        preferred_element_type=jnp.float32,
    )
    code_part = jnp.dot(
        lax.dynamic_slice_in_dim(level_codes, first_row, shard_rows, 1),
        dec_query_w,
        preferred_element_type=jnp.float32,
    )
    agg_query, dec_query = (
        lax.psum(latent_part.astype(jnp.bfloat16), "lat").astype(jnp.float32),
        lax.psum(code_part.astype(jnp.bfloat16), "lat").astype(jnp.float32),
    )
    token_rows = layer_norm(levels_in, norm_gains[0]).reshape(-1, feature_width)
    key_rows, value_rows = fold_pair(
        token_rows,
        (
            lax.all_gather(agg_key_w, "lat", axis=0, tiled=True),
            lax.all_gather(agg_value_w, "lat", axis=0, tiled=True),
        ),
    )
    mixed_rows = attend_levels(key_rows, value_rows.astype(jnp.bfloat16), agg_query, lev_count)
    stacked = stack_queries(mixed_rows)
    projected = fold_single(stacked, lax.all_gather(agg_out_w, "lat", axis=0, tiled=True))
    latent_rows = (
        latents.astype(jnp.float32)[:, None, :]
        + projected.reshape(LATENT, point_count, feature_width)
    ).astype(jnp.bfloat16)
    latent_grid = jnp.concatenate(
        [surface[None], latent_rows.reshape(LATENT, row_count, col_count, feature_width)], axis=0
    )
    for block_id in range(2):
        if block_id == 1:
            latent_grid = roll_forward(latent_grid)
        window_id = window_ids(regions, col_count) if block_id == 1 else None
        grid_rows = latent_grid.reshape(-1, feature_width)
        normed = layer_norm(grid_rows, norm_gains[2 + 2 * block_id])
        packed = fold_single(
            normed, lax.all_gather(qkv_w[block_id], "lat", axis=0, tiled=True)
        ).astype(jnp.bfloat16)
        packed = packed.reshape(ZL, row_count, col_count, 3 * feature_width)
        attended = from_windows(
            window_attention(to_windows(packed), window_id), ZL, row_count, col_count
        ).reshape(-1, feature_width)
        attn_proj = fold_single(
            attended, lax.all_gather(proj_w[block_id], "lat", axis=0, tiled=True)
        )
        after_attention = (grid_rows.astype(jnp.float32) + attn_proj).astype(jnp.bfloat16)
        second = layer_norm(after_attention, norm_gains[3 + 2 * block_id])
        mlp_output = fold_hidden(
            second,
            (
                lax.all_gather(mlp_in[block_id], "lat", axis=0, tiled=True),
                lax.all_gather(mlp_out[block_id], "lat", axis=0, tiled=True),
            ),
        )
        latent_grid = (
            (after_attention.astype(jnp.float32) + mlp_output)
            .astype(jnp.bfloat16)
            .reshape(ZL, row_count, col_count, feature_width)
        )
    returned = roll_back(latent_grid)
    atmos_grid = returned[:LATENT]
    decode_rows = layer_norm(atmos_grid, norm_gains[1]).reshape(-1, feature_width)
    dec_keys, dec_values = fold_pair(
        decode_rows,
        (
            lax.all_gather(dec_key_w, "lat", axis=0, tiled=True),
            lax.all_gather(dec_value_w, "lat", axis=0, tiled=True),
        ),
    )
    decode_mixed = attend_levels(dec_keys, dec_values.astype(jnp.bfloat16), dec_query, LATENT)
    decode_stacked = stack_queries(decode_mixed)
    decode_proj = fold_single(decode_stacked, lax.all_gather(dec_out_w, "lat", axis=0, tiled=True))
    decoded = (
        level_codes.astype(jnp.float32)[:, None, :]
        + decode_proj.reshape(lev_count, point_count, feature_width)
    ).astype(jnp.bfloat16)
    return decoded.reshape(lev_count, row_count, col_count, feature_width)


def solution(mesh):
    in_specs = (
        P(None, "lat", "lon", None),
        P("lat", "lon", None),
        P(),
        P(),
        P(),
        P("lat", None),
        P("lat", None),
        P("lat", None),
        P("lat", None),
        P("lat", None),
        P("lat", None),
        P("lat", None),
        P("lat", None),
        P(None, "lat", None),
        P(None, "lat", None),
        P(None, "lat", None),
        P(None, "lat", None),
        P(None, "lat"),
    )
    out_specs = P(None, "lat", "lon", None)
    return jax.shard_map(body, mesh=mesh, in_specs=in_specs, out_specs=out_specs, check_vma=False)
```

profile of v0, /device:TPU:6, one launch (start us, length us, event | category | flops | bytes accessed | tf_op | source)
XLA Modules:
  0.0 630.3 jit_solution(4380404581988223815)
XLA Ops:
  6.6 1.7 fusion.244
  8.4 1.7 fusion.242
  10.2 1.7 fusion.243
  13.6 0.9 convolution_convert_fusion.4
  14.6 0.7 convert_element_type.207
  15.3 0.9 convolution_convert_fusion.5
  16.3 75.1 %all-reduce = (bf16[16,32,3]{1,0,2:T(8,128)(2,1)S(1)}, bf16[16,32,13]{1,0,2:T(8,128)(2,1)S(1)}) all-reduce(bf16[16,32,3]{1,0,2:T(8,128)(2,1)S(1)} %bitcast.136, bf16[16,32,13]{1,0,2:T(8,128)(2,1)S(1)} %bitcast.135), channel_id=1, replica_groups=mesh['lon'=16,'lat'=16] {'lat'}, use_global_device_ids=true, to_apply=%region_2.0 | all-reduce | flops 8192 | bytes 32768 | tf_op jit(solution)/shard_map/psum | solution.py:202
  92.0 0.6 fusion.6
  93.1 0.6 copy.52
  93.9 45.2 %all_gather.42 = bf16[512,512]{1,0:T(8,128)(2,1)S(1)} all-gather(bf16[32,512]{1,0:T(8,128)(2,1)S(1)} %copy-done.9), channel_id=1, replica_groups=mesh['lon'=16,'lat'=16] {'lat'}, dimensions={0}, use_global_device_ids=true | all-gather | bytes 557056 | tf_op jit(solution)/shard_map/all_gather | solution.py:209
  139.1 0.7 fusion.249
  139.8 1.8 fusion.139
  141.9 1.3 fusion.137
  143.3 38.8 %all_gather.43 = bf16[512,512]{1,0:T(8,128)(2,1)S(1)} all-gather(bf16[32,512]{1,0:T(8,128)(2,1)S(1)} %copy-done.10), channel_id=1, replica_groups=mesh['lon'=16,'lat'=16] {'lat'}, dimensions={0}, use_global_device_ids=true | all-gather | bytes 557056 | tf_op jit(solution)/shard_map/all_gather | solution.py:210
  182.1 1.9 fusion.41
  184.0 1.9 copy.54
  185.9 4.2 reshape.261
  190.2 3.3 copy.55
  193.5 44.1 %all_gather.44 = bf16[512,512]{1,0:T(8,128)(2,1)S(1)} all-gather(bf16[32,512]{1,0:T(8,128)(2,1)S(1)} %copy-done.11), channel_id=1, replica_groups=mesh['lon'=16,'lat'=16] {'lat'}, dimensions={0}, use_global_device_ids=true | all-gather | bytes 557056 | tf_op jit(solution)/shard_map/all_gather | solution.py:215
  237.6 1.3 multiply_reduce_fusion.1
  240.2 38.7 %all-gather.1 = bf16[1,512,512]{2,1,0:T(8,128)(2,1)S(1)} all-gather(bf16[1,32,512]{2,1,0:T(8,128)(2,1)S(1)} %get-tuple-element.28), channel_id=3, replica_groups=mesh['lon'=16,'lat'=16] {'lat'}, dimensions={1}, use_global_device_ids=true | all-gather | bytes 557056 | tf_op jit(solution)/shard_map/all_gather | solution.py:237
  279.0 43.6 %all-gather.5 = bf16[1,512,512]{2,1,0:T(8,128)(2,1)S(1)} all-gather(bf16[1,32,512]{2,1,0:T(8,128)(2,1)S(1)} %get-tuple-element.27), channel_id=7, replica_groups=mesh['lon'=16,'lat'=16] {'lat'}, dimensions={1}, use_global_device_ids=true | all-gather | bytes 557056 | tf_op jit(solution)/shard_map/all_gather | solution.py:237
  322.8 1.4 mul.307
  324.2 2.1 convolution_convert_fusion.1
  326.8 1.0 copy.57
  327.8 1.1 fusion.2
  328.9 1.0 fusion.53
  329.9 0.6 copy.61
  331.5 8.3 %fusion.57 = bf16[288,512]{1,0:T(8,128)(2,1)S(1)} fusion(f32[288,512]{1,0:T(8,128)S(1)} %get-tuple-element.38, bf16[1,2048,512]{2,1,0:T(8,128)(2,1)} %all-gather.19.cloned.1.call-done, bf16[1,2048,512]{2,1,0:T(8,128)(2,1)} %all-gather.17.cloned.1.call-done, f32[512]{0:T(512)S(1)} %bitcast.141, f32[288]{0:T(512)S(1)} %add_rsqrt_fusion.5, ...), kind=kOutput, calls=%fused_computation.83 | convolution fusion | flops 1247182848 | bytes 5083392 | tf_op jit(solution)/shard_map/dot_general | solution.py:128
  340.6 41.2 %all_gather.53 = bf16[512,512]{1,0:T(8,128)(2,1)} all-gather(bf16[32,512]{1,0:T(8,128)(2,1)S(1)} %copy-done.12), channel_id=1, replica_groups=mesh['lon'=16,'lat'=16] {'lat'}, dimensions={0}, use_global_device_ids=true | all-gather | bytes 557056 | tf_op jit(solution)/shard_map/all_gather | solution.py:259
  381.9 12.2 %collective-permute-start.1 = (bf16[4,3,12,512]{3,2,1,0:T(8,128)(2,1)S(1)}, bf16[4,3,12,512]{3,2,1,0:T(8,128)(2,1)S(1)}, u32[]{:S(2)}, u32[]{:S(2)}) collective-permute-start(bf16[4,3,12,512]{3,2,1,0:T(8,128)(2,1)S(1)} %get-tuple-element.18), channel_id=1, source_target_pairs={{1,0},{2,1},{3,2},{4,3},{5,4},{6,5},{7,6},{8,7},{9,8},{10,9},{11,1... | collective-permute-start | bytes 442376 | tf_op jit(solution)/shard_map/ppermute | solution.py:22
  394.2 4.6 collective-permute-done.1
  399.7 2.1 convolution_convert_fusion
  402.2 1.0 copy.62
  403.2 1.3 fusion.3
  404.5 1.2 fusion.52
  405.7 0.5 copy.66
  407.3 30.3 %all-gather.23.cloned.1.call-done = bf16[1,2048,512]{2,1,0:T(8,128)(2,1)} async-done(((bf16[1,128,512]{2,1,0:T(8,128)(2,1)}), bf16[1,2048,512]{2,1,0:T(8,128)(2,1)}) %all-gather.23.cloned.1.call-update) | async-done | bytes 2097168 | tf_op jit(solution)/shard_map/all_gather | solution.py:244
  437.5 84.7 %all-gather.25.cloned.1.call-done = bf16[1,2048,512]{2,1,0:T(8,128)(2,1)} async-done(((bf16[1,128,512]{2,1,0:T(8,128)(2,1)}), bf16[1,2048,512]{2,1,0:T(8,128)(2,1)}) %all-gather.25.cloned.1.call-update) | async-done | bytes 2097168 | tf_op jit(solution)/shard_map/all_gather | solution.py:245
  522.2 8.3 %fusion.54 = bf16[288,512]{1,0:T(8,128)(2,1)S(1)} fusion(f32[288,512]{1,0:T(8,128)S(1)} %get-tuple-element.42, bf16[1,2048,512]{2,1,0:T(8,128)(2,1)} %all-gather.25.cloned.1.call-done, bf16[1,2048,512]{2,1,0:T(8,128)(2,1)} %all-gather.23.cloned.1.call-done, f32[512]{0:T(512)S(1)} %bitcast.139, f32[288]{0:T(512)S(1)} %add_rsqrt_fusion.4, ...), kind=kOutput, calls=%fused_computation.82 | convolution fusion | flops 1247182848 | bytes 5083392 | tf_op jit(solution)/shard_map/dot_general | solution.py:128
  530.7 2.9 collective-permute-start.2
  533.7 40.2 %all_gather.54 = bf16[512,512]{1,0:T(8,128)(2,1)S(1)} all-gather(bf16[32,512]{1,0:T(8,128)(2,1)S(1)} %copy-done.13), channel_id=1, replica_groups=mesh['lon'=16,'lat'=16] {'lat'}, dimensions={0}, use_global_device_ids=true | all-gather | bytes 557056 | tf_op jit(solution)/shard_map/all_gather | solution.py:260
  574.1 42.3 %all_gather.55 = bf16[512,512]{1,0:T(8,128)(2,1)S(1)} all-gather(bf16[32,512]{1,0:T(8,128)(2,1)S(1)} %copy-done.14), channel_id=1, replica_groups=mesh['lon'=16,'lat'=16] {'lat'}, dimensions={0}, use_global_device_ids=true | all-gather | bytes 557056 | tf_op jit(solution)/shard_map/all_gather | solution.py:265
  617.3 0.6 fusion.138
  619.1 0.7 copy.69
  619.8 1.3 multiply_reduce_fusion
  621.2 0.7 add_convert_fusion
  621.9 1.3 copy.78
  (137 shorter events, 12.3 us)
Async XLA Ops:
  6.5 7.1 %copy-start = (bf16[32,512]{1,0:T(8,128)(2,1)S(1)}, bf16[32,512]{1,0:T(8,128)(2,1)}, u32[]{:S(2)}) copy-start(bf16[32,512]{1,0:T(8,128)(2,1)} %param.27) | copy-start | bytes 98308
  6.5 8.8 %copy-start.15 = (bf16[32,512]{1,0:T(8,128)(2,1)S(1)}, bf16[32,512]{1,0:T(8,128)(2,1)}, u32[]{:S(2)}) copy-start(bf16[32,512]{1,0:T(8,128)(2,1)} %param.23) | copy-start | bytes 98308
  6.5 85.1 %copy-start.17 = (f32[6,512]{1,0:T(8,128)S(1)}, f32[6,512]{1,0:T(8,128)}, u32[]{:S(2)}) copy-start(f32[6,512]{1,0:T(8,128)} %param.22) | copy-start | bytes 36868
  6.5 85.2 %copy-start.2 = (bf16[13,6,12,512]{3,0,2,1:T(8,128)(2,1)S(1)}, bf16[13,6,12,512]{3,0,2,1:T(8,128)(2,1)}, u32[]{:S(2)}) copy-start(bf16[13,6,12,512]{3,0,2,1:T(8,128)(2,1)} %param.18) | copy-start | bytes 2875396
  6.5 317.7 %all-gather.15.cloned.1.call-start = ((), (), s32[]{:S(2)}) async-start(), calls=%async_computation | async-start | bytes 1671168 | tf_op jit(solution)/shard_map/all_gather | solution.py:230
  8.3 323.1 %all-gather.17.cloned.1.call-start = ((), (), s32[]{:S(2)}) async-start(), calls=%async_computation.1 | async-start | bytes 2228224 | tf_op jit(solution)/shard_map/all_gather | solution.py:244
  10.1 321.4 %all-gather.19.cloned.1.call-start = ((), (), s32[]{:S(2)}) async-start(), calls=%async_computation.2 | async-start | bytes 2228224 | tf_op jit(solution)/shard_map/all_gather | solution.py:245
  11.9 387.8 %all-gather.21.cloned.1.call-start = ((), (), s32[]{:S(2)}) async-start(), calls=%async_computation.3 | async-start | bytes 1671168 | tf_op jit(solution)/shard_map/all_gather | solution.py:230
  12.5 425.1 %all-gather.23.cloned.1.call-start = ((), (), s32[]{:S(2)}) async-start(), calls=%async_computation.4 | async-start | bytes 2228224 | tf_op jit(solution)/shard_map/all_gather | solution.py:244
  13.0 509.2 %all-gather.25.cloned.1.call-start = ((), (), s32[]{:S(2)}) async-start(), calls=%async_computation.5 | async-start | bytes 2228224 | tf_op jit(solution)/shard_map/all_gather | solution.py:245
  93.0 0.8 copy-start.9
  139.8 3.5 copy-start.10
  190.2 3.3 copy-start.11
  237.6 1.8 copy-start.5
  238.9 1.0 copy-start.16
  238.9 1.2 copy-start.8
  239.3 39.6 %copy-start.18 = (s32[4,6]{1,0:T(4,128)S(1)}, s32[4,6]{1,0:T(4,128)}, u32[]{:S(2)}) copy-start(s32[4,6]{1,0:T(4,128)} %param.35) | copy-start | bytes 292
  327.8 1.1 copy-start.7
  339.8 0.8 copy-start.12
  340.1 41.7 %collective-permute-start = (bf16[4,6,6,512]{3,2,1,0:T(8,128)(2,1)S(1)}, bf16[4,6,6,512]{3,2,1,0:T(8,128)(2,1)S(1)}, u32[]{:S(2)}, u32[]{:S(2)}) collective-permute-start(bf16[4,6,6,512]{3,2,1,0:T(8,128)(2,1)S(1)} %get-tuple-element.20), channel_id=1, source_target_pairs={{16,0},{32,16},{48,32},{64,48},{80,64},{96,80},{112,96},{128,112},... | collective-permute-start | bytes 442376 | tf_op jit(solution)/shard_map/ppermute | solution.py:22
  381.9 16.9 %collective-permute-start.1 = (bf16[4,3,12,512]{3,2,1,0:T(8,128)(2,1)S(1)}, bf16[4,3,12,512]{3,2,1,0:T(8,128)(2,1)S(1)}, u32[]{:S(2)}, u32[]{:S(2)}) collective-permute-start(bf16[4,3,12,512]{3,2,1,0:T(8,128)(2,1)S(1)} %get-tuple-element.18), channel_id=1, source_target_pairs={{1,0},{2,1},{3,2},{4,3},{5,4},{6,5},{7,6},{8,7},{9,8},{10,9},{11,1... | collective-permute-start | bytes 442376 | tf_op jit(solution)/shard_map/ppermute | solution.py:22
  403.2 1.3 copy-start.6
  522.2 11.4 %copy-start.13 = (bf16[32,512]{1,0:T(8,128)(2,1)S(1)}, bf16[32,512]{1,0:T(8,128)(2,1)}, u32[]{:S(2)}) copy-start(bf16[32,512]{1,0:T(8,128)(2,1)} %param.29) | copy-start | bytes 98308
  530.6 43.5 %copy-start.14 = (bf16[32,512]{1,0:T(8,128)(2,1)S(1)}, bf16[32,512]{1,0:T(8,128)(2,1)}, u32[]{:S(2)}) copy-start(bf16[32,512]{1,0:T(8,128)(2,1)} %param.30) | copy-start | bytes 98308
  530.7 86.4 %copy-start.3 = (bf16[512,512]{1,0:T(8,128)(2,1)S(1)}, bf16[512,512]{1,0:T(8,128)(2,1)}, u32[]{:S(2)}) copy-start(bf16[512,512]{1,0:T(8,128)(2,1)} %all_gather.53) | copy-start | bytes 1572868
  530.7 43.2 %collective-permute-start.2 = (bf16[4,3,12,512]{3,2,1,0:T(8,128)(2,1)S(1)}, bf16[4,3,12,512]{3,2,1,0:T(8,128)(2,1)S(1)}, u32[]{:S(2)}, u32[]{:S(2)}) collective-permute-start(bf16[4,3,12,512]{3,2,1,0:T(8,128)(2,1)S(1)} %get-tuple-element.15), channel_id=1, source_target_pairs={{15,0},{0,1},{1,2},{2,3},{3,4},{4,5},{5,6},{6,7},{7,8},{8,9},{9,10... | collective-permute-start | bytes 442376 | tf_op jit(solution)/shard_map/ppermute | solution.py:22
  573.9 43.4 %copy-start.4 = (f32[512,208]{0,1:T(8,128)S(1)}, f32[512,208]{0,1:T(8,128)}, u32[]{:S(2)}) copy-start(f32[512,208]{0,1:T(8,128)} %mul.307) | copy-start | bytes 1277956
  574.0 42.4 %collective-permute-start.3 = (bf16[4,6,6,512]{3,2,1,0:T(8,128)(2,1)S(1)}, bf16[4,6,6,512]{3,2,1,0:T(8,128)(2,1)S(1)}, u32[]{:S(2)}, u32[]{:S(2)}) collective-permute-start(bf16[4,6,6,512]{3,2,1,0:T(8,128)(2,1)S(1)} %fusion.167), channel_id=1, source_target_pairs={{240,0},{0,16},{16,32},{32,48},{48,64},{64,80},{80,96},{96,112},{1... | collective-permute-start | bytes 442376 | tf_op jit(solution)/shard_map/ppermute | solution.py:22
  621.2 2.1 copy-start.1
Sparse Core Ops, SparseCore 0:
  10.0 83.7 all-gather.14
  96.4 86.0 all-gather.16
  185.1 86.5 all-gather.18
  274.1 78.7 all-gather.20
  355.3 82.1 all-gather.22
  440.0 82.2 all-gather.24
where the time goes:
time: 639 us; the launch traced here: 630 us
  blocking collectives  409 us (64%)
  waiting for transfers between devices  121 us (19%)
  matrix products  34.5 us (5%)
  local copies, waits for them, and re-layouts  26.4 us (4%)
  starting transfers between devices  15.5 us (2%)
  between operations  14.5 us (2%)
  other arithmetic  8.97 us (1%)
    all_gather x2, waiting for transfers between devices, body(): lax.all_gather(mlp_out[block_id], 'lat', axis=0, tiled=True)  84.7 us
    all_gather x2, blocking collectives, body(): lax.all_gather(proj_w[block_id], 'lat', axis=0, tiled=True)  82.2 us
    psum x1, blocking collectives, body(): lax.psum(latent_part.astype(jnp.bfloat16), 'lat').astype(jnp.float32)  75.1 us
    all_gather x1, blocking collectives, body(): lax.all_gather(agg_key_w, 'lat', axis=0, tiled=True)  45.2 us
    all_gather x1, blocking collectives, body(): lax.all_gather(agg_out_w, 'lat', axis=0, tiled=True)  44.1 us
    all_gather x1, blocking collectives, body(): lax.all_gather(dec_out_w, 'lat', axis=0, tiled=True)  42.3 us
    all_gather x1, blocking collectives, body(): lax.all_gather(dec_key_w, 'lat', axis=0, tiled=True)  41.2 us
    all_gather x1, blocking collectives, body(): lax.all_gather(dec_value_w, 'lat', axis=0, tiled=True)  40.2 us
  transfers between devices with their start and end apart: 10, of which 3 were waited for; matrix products, arithmetic and copies ran while one was open for 8% of the time, Pallas kernels for 0%

commit v1 on v0

v1 whole, which is shorter than its diff:
```python
import functools

import jax
import jax.numpy as jnp
import numpy as np
from jax import lax
from jax.experimental import pallas as pl
from jax.experimental.pallas import tpu as pltpu
from jax.sharding import PartitionSpec as P

LEVELS = 13
LATENT = 3
HEADS = 16
HD = 32
D = 512
PATCHES = 72
TOKENS = 288
WINDOW = 144
ROWS = 960
SCALE = HD ** (-0.5)
EPSILON = 1e-05
F32 = jnp.float32
BF16 = jnp.bfloat16

CHUNKS = (
    ((("agg_query_w", None), ("agg_key_w", None)), 32, 512, 0, "xy"),
    ((("agg_value_w", None), ("agg_out_w", None)), 32, 512, 1, "yx"),
    ((("qkv_w", 0),), 32, 1536, 0, "xy"),
    ((("proj_w", 0),), 32, 512, 1, "yx"),
    ((("mlp_in", 0),), 128, 512, 0, "xy"),
    ((("mlp_out", 0),), 128, 512, 1, "yx"),
    ((("proj_w", 1),), 32, 512, 0, "xy"),
    ((("qkv_w", 1),), 32, 1536, 1, "yx"),
    ((("mlp_in", 1),), 128, 512, 0, "z"),
    ((("mlp_out", 1),), 128, 512, 1, "z"),
    ((("dec_query_w", None), ("dec_key_w", None)), 32, 512, 0, "xy"),
    ((("dec_value_w", None), ("dec_out_w", None)), 32, 512, 1, "yx"),
)
WEIGHTS = ("agg_query_w", "agg_key_w", "agg_value_w", "agg_out_w", "dec_query_w", "dec_key_w",
           "dec_value_w", "dec_out_w", "qkv_w", "proj_w", "mlp_in", "mlp_out")
ALL = slice(None)


def buffer_shape(chunk):
    return (len(chunk[0]), 8, 2, 2, chunk[1] // 2, chunk[2])


class Place:
    def __init__(self):
        lat, lon = lax.axis_index("lat"), lax.axis_index("lon")
        self.lat, self.lon = lat, lon
        self.z, self.h = lax.div(lat, 2), lax.rem(lat, 2)
        self.y, self.l, self.core = lax.div(lon, 4), lax.rem(lax.div(lon, 2), 2), lax.rem(lon, 2)
        self.x = 2 * self.h + self.l

    def device(self, z=None, x=None, y=None, core=None):
        z = self.z if z is None else z
        x = self.x if x is None else x
        y = self.y if y is None else y
        core = self.core if core is None else core
        return {"lat": 2 * z + lax.div(x, 2), "lon": 4 * y + 2 * lax.rem(x, 2) + core}

    def beside(self, lat_step, lon_step):
        return {"lat": lax.rem(self.lat + lat_step + 16, 16), "lon": lax.rem(self.lon + lon_step + 16, 16)}

    def turn(self, axis, step):
        size = 8 if axis == "z" else 4
        return lax.rem(getattr(self, axis) + step + size, size)


def remote(src, dst, send_sem, recv_sem, device):
    return pltpu.make_async_remote_copy(src_ref=src, dst_ref=dst, send_sem=send_sem, recv_sem=recv_sem,
                                        device_id=device, device_id_type=pl.DeviceIdType.MESH)


def wait_bytes(ref, sem):
    pltpu.make_async_copy(ref, ref, sem).wait()


class Carrier:
    def __init__(self, place, chunk, sources, buf, index, send, recv, core_recv):
        self.place, self.chunk, self.sources, self.buf, self.index = place, chunk, sources, buf, index
        self.send, self.recv, self.core_recv = send, recv, core_recv
        self.core, self.kind = chunk[3], chunk[4]
        self.last = 5 if self.kind == "z" else 4
        self.done = 0

    def cols(self, y):
        width = self.chunk[2] // 4
        return pl.ds(pl.multiple_of(y * width, 128), width)

    def part(self, stage, c, zs=ALL):
        d1, d2 = self.kind
        at = {d2: c}
        if stage == 1:
            at = {d1: c, d2: getattr(self.place, d2)}
        x, y = at.get("x"), at.get("y")
        hl = (ALL, ALL) if x is None else (lax.div(x, 2), lax.rem(x, 2))
        return self.buf.at[(ALL, zs) + hl + (ALL, ALL if y is None else self.cols(y))]

    def to(self, ref, slot, **where):
        return remote(ref, ref, self.send.at[self.index, slot], self.recv.at[self.index, slot],
                      self.place.device(**where))

    def to_core(self, ref, k):
        return remote(ref, ref, self.send.at[self.index, 9 + k], self.core_recv.at[self.index, k],
                      self.place.device(core=1 - self.place.core))

    def first_copies(self):
        p, half = self.place, self.chunk[1] // 2
        local, away = [], []
        for k, src in enumerate(self.sources):
            if self.kind == "z":
                for n in range(2):
                    s, d = src.at[pl.ds(n * half, half)], self.buf.at[k, p.z, p.h, n]
                    local.append(pltpu.make_async_copy(s, d, self.send.at[self.index, 17]))
                    away.append(remote(s, d, self.send.at[self.index, 0], self.recv.at[self.index, 0],
                                       p.device(x=lax.rem(p.x + 3 + 2 * p.l, 4))))
            else:
                s = src.at[pl.ds(pl.multiple_of(p.l * half, 16), half), self.cols(p.y)]
                d = self.buf.at[k, p.z, p.h, p.l, :, self.cols(p.y)]
                local.append(pltpu.make_async_copy(s, d, self.send.at[self.index, 17]))
                for step in range(1, 8):
                    away.append(remote(s, d, self.send.at[self.index, 0], self.recv.at[self.index, 0],
                                       p.device(z=p.turn("z", step))))
        return local, away

    def first_size(self):
        p = self.place
        if self.kind == "z":
            return self.buf.at[:, p.z, p.h]
        return self.buf.at[:, pl.ds(0, 7), p.h, p.l, :, self.cols(p.y)]

    def copies(self, task):
        p = self.place
        if self.kind == "z":
            if task == 1:
                own = self.buf.at[:, p.z]
                return [(None, self.to(own, 1, z=p.turn("z", 1))), (None, self.to(own, 2, z=p.turn("z", -1))),
                        (None, self.to_core(own, 0))]
            if task == 5:
                far = p.turn("z", 4)
                return [((self.buf.at[:, far, 0], 7), None), ((self.buf.at[:, far, 1], 8), None),
                        (None, self.to_core(self.buf.at[:, far], 7))]
            found = []
            for n, sign in enumerate((1, -1)):
                c = p.turn("z", sign * (1 - task))
                slab = self.buf.at[:, c]
                onward = self.buf.at[:, c, n] if task == 4 else slab
                found.append(((slab, 2 * task - 3 + n), self.to(onward, 2 * task - 1 + n, z=p.turn("z", sign))))
                found.append((None, self.to_core(slab, 2 * task - 3 + n)))
            return found
        d1, d2 = self.kind
        if task == 1:
            own = self.part(1, getattr(p, d1))
            return [(None, self.to(own, 1, **{d1: p.turn(d1, 1)})), (None, self.to(own, 2, **{d1: p.turn(d1, -1)})),
                    (None, self.to(own, 3, **{d1: p.turn(d1, 2)}))]
        up, down, far = p.turn(d2, 1), p.turn(d2, -1), p.turn(d2, 2)
        low, high = pl.ds(0, 4), pl.ds(4, 4)
        if task == 2:
            own = self.part(2, getattr(p, d2))
            return [((self.part(1, p.turn(d1, -1)), 1), None), ((self.part(1, p.turn(d1, 1)), 2), None),
                    ((self.part(1, p.turn(d1, 2)), 3), None),
                    (None, self.to(own, 5, **{d2: up})), (None, self.to(own, 6, **{d2: down})),
                    (None, self.to_core(own, 0))]
        if task == 3:
            return [((self.part(2, down), 5), self.to(self.part(2, down, low), 7, **{d2: up})),
                    ((self.part(2, up), 6), self.to(self.part(2, up, high), 8, **{d2: down})),
                    (None, self.to_core(self.part(2, down), 1)), (None, self.to_core(self.part(2, up), 2))]
        return [((self.part(2, far, low), 7), None), ((self.part(2, far, high), 8), None),
                (None, self.to_core(self.part(2, far), 3))]

    def run(self, task):
        assert task == self.done, (self.chunk, task)
        self.done += 1

        @pl.when(self.place.core == self.core)
        def _():
            p = self.place
            if task == 0:
                local, away = self.first_copies()
                for copy in away + local:
                    copy.start()
                return
            if task == 1:
                own = self.buf.at[:, p.z, p.h]
                if self.kind != "z":
                    own = self.buf.at[:, p.z, p.h, p.l, :, self.cols(p.y)]
                wait_bytes(own, self.send.at[self.index, 17])
                wait_bytes(self.first_size(), self.recv.at[self.index, 0])
            for before, copy in self.copies(task):
                if before is not None:
                    wait_bytes(before[0], self.recv.at[self.index, before[1]])
                if copy is not None:
                    copy.start()

    def finish(self):
        @pl.when(self.place.core == self.core)
        def _():
            wait_bytes(self.first_size(), self.send.at[self.index, 0])
            for task in range(1, self.last + 1):
                for _, copy in self.copies(task):
                    if copy is not None:
                        copy.wait_send()

    def arrived(self):
        assert self.done == self.last + 1, self.chunk
        p = self.place

        @pl.when(p.core != self.core)
        def _():
            if self.kind == "z":
                refs = [self.buf.at[:, p.turn("z", n)] for n in (0, -1, 1, -2, 2, -3, 3, 4)]
            else:
                d2 = self.kind[1]
                refs = [self.part(2, p.turn(d2, n)) for n in (0, -1, 1, 2)]
            for k, ref in enumerate(refs):
                wait_bytes(ref, self.core_recv.at[self.index, k])


def normed(values, gain):
    centre = values - jnp.mean(values, axis=-1, keepdims=True)
    variance = jnp.mean(centre * centre, axis=-1, keepdims=True)
    return (centre * lax.rsqrt(variance + EPSILON) * gain).astype(BF16)


def dot(a, b):
    return jnp.dot(a, b, preferred_element_type=F32)


def dot_t(a, b):
    return lax.dot_general(a, b, (((1,), (1,)), ((), ())), preferred_element_type=F32)


def gelu(values):
    return (0.5 * values * (1.0 + lax.erf(values * (0.5 ** 0.5)))).astype(BF16)


def rounded(values):
    return values.astype(BF16).astype(F32)


def split(values):
    high = values.astype(BF16)
    return high, (values - high.astype(F32)).astype(BF16)


def lane_head(shape):
    return lax.div(lax.broadcasted_iota(jnp.int32, shape, len(shape) - 1), HD)


def head_rows(queries, count):
    own = lax.broadcasted_iota(jnp.int32, (HEADS, D), 0) == lane_head((HEADS, D))
    return jnp.concatenate([jnp.where(own, queries[n:n + 1], 0.0) for n in range(count)], axis=0)


def spread_matrix(rows, first):
    shape = (rows, D)
    own = lax.broadcasted_iota(jnp.int32, shape, 0) - first == lane_head(shape)
    return jnp.where(own, 1.0, 0.0).astype(BF16)


def score_matrix(queries, count, query_w, key_w, high_ref, low_ref):
    high, low = split(head_rows(dot(queries, query_w), count))
    high_ref[...], low_ref[...] = split(dot_t(key_w, high) + dot_t(key_w, low))


def rows_of(index, size):
    return pl.ds(pl.multiple_of(index * size, size & -size), size)


def norm_rows(src, dst, gain, rows, block=48):
    def step(n, _):
        dst[rows_of(n, block)] = normed(src[rows_of(n, block)], gain)
        return 0
    lax.fori_loop(0, rows // block, step, 0, unroll=True)


def attention(packed, attended, masks):
    lane = lane_head((WINDOW, 128))
    ones = jnp.ones((WINDOW, 128), BF16)

    def step(n, _):
        w, g = lax.div(n, 4), lax.rem(n, 4)
        rows = rows_of(w, WINDOW)
        q, k, v = (packed[rows, pl.ds(pl.multiple_of(g * 128 + part * D, 128), 128)] for part in range(3))
        heads = [jnp.where(lane == m, q, jnp.zeros_like(q)) for m in range(4)]
        weights = []
        for m in range(4):
            e = jnp.exp(dot_t(heads[m], k) * SCALE)
            if masks is not None:
                e = e * masks[w]
            weights.append(e.astype(BF16))
        both = jnp.concatenate([v, ones], axis=1)
        total = jnp.zeros((WINDOW, 128), F32)
        for m in range(4):
            mixed = dot(weights[m], both)
            total = jnp.where(lane == m, mixed[:, :128] / mixed[:, 128:], total)
        attended[rows, pl.ds(pl.multiple_of(g * 128, 128), 128)] = total.astype(BF16)
        return 0
    lax.fori_loop(0, 8, step, 0)


def kernel(plan, *refs):
    (levels_ref, surface_ref, latents_ref, codes_ref, gains_ref, regions_ref), refs = refs[:6], refs[6:]
    sources, refs = dict(zip(WEIGHTS, refs[:12])), refs[12:]
    (pack1, open1, pack2, open2), refs = refs[:4], refs[4:]
    out_ref, refs = refs[0], refs[1:]
    buffers, refs = refs[:len(CHUNKS)], refs[len(CHUNKS):]
    (send, recv, core_recv, halo_send, halo_recv, stage, norm, values, expo, fa_high, fa_low, fd_high, fd_low,
     grid, packed, attended, grid_norm, total, masks, out1, in1, out2, in2, dec_expo) = refs

    place = Place()
    barrier = pltpu.get_barrier_semaphore()
    friends = [place.device(z=place.turn("z", n)) for n in range(1, 8)]
    friends += [place.device(x=place.turn("x", n)) for n in range(1, 4)]
    friends += [place.device(y=place.turn("y", n)) for n in range(1, 4)]
    friends += [place.device(core=1 - place.core)]
    friends += [place.beside(i, j) for i, j in ((1, 0), (0, 1), (1, 1), (-1, 0), (0, -1), (-1, -1))]
    for friend in friends:
        pl.semaphore_signal(barrier, inc=1, device_id=friend, device_id_type=pl.DeviceIdType.MESH)
    pl.semaphore_wait(barrier, len(friends))

    carriers, count = [], [0, 0]
    for chunk, buf in zip(CHUNKS, buffers):
        own = [sources[w] if k is None else sources[w].at[k] for w, k in chunk[0]]
        carriers.append(Carrier(place, chunk, own, buf, count[chunk[3]], send, recv, core_recv))
        count[chunk[3]] += 1
    pairs = list(zip(carriers[0::2], carriers[1::2]))

    def pump(point):
        for pair, task in plan.get(point, ()):
            for carrier in pairs[pair]:
                carrier.run(task)

    def weight(n, k=0):
        buf = buffers[n]
        return buf[k].reshape(16 * CHUNKS[n][1], CHUNKS[n][2])

    def ready(*numbers):
        for n in numbers:
            carriers[n].arrived()

    pump("start")
    stage[936:960] = jnp.zeros((24, D), F32)
    for level in range(LEVELS):
        for i in range(6):
            stage[PATCHES * level + 12 * i:PATCHES * level + 12 * i + 12] = levels_ref[level, i].astype(F32)
    for i in range(6):
        grid[12 * i:12 * i + 12] = surface_ref[i].astype(F32)
    pump("compact")
    norm_rows(stage, norm, gains_ref[0:1], ROWS)
    pump("norm")
    ready(0)
    score_matrix(latents_ref[...], LATENT, weight(0, 0), weight(0, 1), fa_high, fa_low)
    pump("agg_matrix")

    def score_step(n, _):
        block = norm[rows_of(n, 192)]
        expo[rows_of(n, 192)] = jnp.exp((dot(block, fa_high[...]) + dot(block, fa_low[...])) * SCALE)
        return 0
    lax.fori_loop(0, ROWS // 192, score_step, 0)
    pump("agg_scores")
    ready(1)

    def value_step(n, _):
        values[rows_of(n, 192)] = dot(norm[rows_of(n, 192)], weight(1, 0))
        return 0
    lax.fori_loop(0, ROWS // 192, value_step, 0)
    pump("agg_values")
    inverse = 1.0 / lax.fori_loop(
        0, LEVELS, lambda n, s: s + expo[rows_of(n, PATCHES)], jnp.zeros((PATCHES, LATENT * HEADS), F32))
    for a in range(LATENT):
        spread = spread_matrix(LATENT * HEADS, HEADS * a)

        def mix_step(n, s):
            probs = (expo[rows_of(n, PATCHES)] * inverse).astype(BF16)
            return s + dot(probs, spread) * values[rows_of(n, PATCHES)]
        mixed = lax.fori_loop(0, LEVELS, mix_step, jnp.zeros((PATCHES, D), F32))
        total[PATCHES * a:PATCHES * a + PATCHES] = mixed
        pump("agg_mix%d" % a)
    projected = dot(total[0:216].astype(BF16), weight(1, 1))
    for a in range(LATENT):
        rows = projected[PATCHES * a:PATCHES * a + PATCHES]
        grid[PATCHES * (a + 1):PATCHES * (a + 2)] = rounded(latents_ref[a:a + 1].astype(F32) + rows)
    pump("agg_out")

    def block(b):
        name = "b%d_" % b
        norm_rows(grid, grid_norm, gains_ref[2 + 2 * b:3 + 2 * b], TOKENS)
        qkv_n, proj_n = (7, 6) if b else (2, 3)
        in_n, out_n = (8, 9) if b else (4, 5)
        ready(qkv_n)
        for n in range(6):
            cols = buffers[qkv_n][0, :, :, :, :, 256 * n:256 * n + 256].reshape(D, 256)
            packed[:, 256 * n:256 * n + 256] = dot(grid_norm[...], cols).astype(BF16)
        pump(name + "qkv")
        attention(packed, attended, masks if b else None)
        pump(name + "attention")
        ready(proj_n)
        grid[...] = rounded(grid[...] + dot(attended[...], weight(proj_n)))
        pump(name + "proj")
        norm_rows(grid, grid_norm, gains_ref[3 + 2 * b:4 + 2 * b], TOKENS)
        ready(in_n, out_n)
        total[...] = grid[...]

        def step(n, _):
            hidden = gelu(dot_t(grid_norm[...], buffers[in_n][0, n].reshape(256, D)))
            total[...] += dot(hidden, buffers[out_n][0, n].reshape(256, D))
            return 0
        for part in range(4):
            lax.fori_loop(2 * part, 2 * part + 2, step, 0)
            pump(name + "mlp%d" % part)

    block(0)

    def exchange(source, target, size, slot, own, sends):
        keep = pltpu.make_async_copy(source.at[pl.ds(own * size, size)], target.at[pl.ds(own * size, size)],
                                     halo_send.at[slot, 3])
        copies = [remote(source.at[pl.ds(q * size, size)], target.at[pl.ds(q * size, size)], halo_send.at[slot, n],
                         halo_recv.at[slot, n], place.beside(i, j)) for n, (q, i, j) in enumerate(sends)]
        for copy in copies:
            copy.start()
        keep.start()
        return copies, keep

    out1[...] = dot(pack1[...], total[...].astype(BF16)).astype(BF16)
    copies, keep = exchange(out1, in1, 80, 0, 3, ((1, -1, 0), (2, 0, -1), (0, -1, -1)))
    pump("halo1")
    ids = [[regions_ref[level, i] for i in range(6)] for level in range(4)]
    for w in range(2):
        rows_id = jnp.zeros((WINDOW, WINDOW), jnp.int32)
        cols_id = jnp.zeros((WINDOW, WINDOW), jnp.int32)
        for n in range(12):
            value = ids[2 * w + n // 6][n % 6]
            rows_id = jnp.where(lax.broadcasted_iota(jnp.int32, (WINDOW, WINDOW), 0) >= 12 * n, value, rows_id)
            cols_id = jnp.where(lax.broadcasted_iota(jnp.int32, (WINDOW, WINDOW), 1) >= 12 * n, value, cols_id)
        masks[w] = jnp.where(rows_id == cols_id, 1.0, 0.0)
    for copy in copies:
        copy.wait()
    keep.wait()
    grid[...] = dot(open1[...], in1[...])
    block(1)
    out2[...] = dot(pack2[...], total[...].astype(BF16)).astype(BF16)
    copies, keep = exchange(out2, in2, 64, 1, 0, ((2, 1, 0), (1, 0, 1), (3, 1, 1)))
    pump("halo2")
    ready(10)
    score_matrix(codes_ref[...], LEVELS, weight(10, 0), weight(10, 1), fd_high, fd_low)
    for copy in copies:
        copy.wait()
    keep.wait()
    atmos = normed(dot(open2[...], in2[...]), gains_ref[1:2])
    expos = jnp.exp((dot(atmos, fd_high[...]) + dot(atmos, fd_low[...])) * SCALE)
    inverse = 1.0 / (expos[:PATCHES] + expos[PATCHES:2 * PATCHES] + expos[2 * PATCHES:])
    dec_expo[...] = expos * jnp.concatenate([inverse] * LATENT, axis=0)
    ready(11)
    total[0:216] = dot(atmos, weight(11, 0))

    def decode_step(n, _):
        spread = spread_matrix(LEVELS * HEADS, HEADS * n)
        wide = dot(dec_expo[...].astype(BF16), spread) * total[0:216]
        stage[rows_of(n, PATCHES)] = wide[:PATCHES] + wide[PATCHES:2 * PATCHES] + wide[2 * PATCHES:]
        return 0
    lax.fori_loop(0, LEVELS, decode_step, 0)

    def out_step(n, _):
        values[rows_of(n, 192)] = dot(stage[rows_of(n, 192)].astype(BF16), weight(11, 1))
        return 0
    lax.fori_loop(0, ROWS // 192, out_step, 0)
    for level in range(LEVELS):
        code = codes_ref[level:level + 1].astype(F32)
        for i in range(6):
            rows = values[PATCHES * level + 12 * i:PATCHES * level + 12 * i + 12]
            out_ref[level, i] = (code + rows).astype(BF16)
    for carrier in carriers:
        carrier.finish()


def one_hot(targets, sources):
    return (np.asarray(targets)[:, None] == np.arange(sources)[None, :]).astype(np.float32)


def permutations():
    pack_a, open_a, pack_b, open_b = [], [], [], []
    for q in range(4):
        for t in range(80):
            z, i, j = t // 18, t % 18 // 6, t % 6
            pack_a.append(z * 72 + (3 * (q // 2) + i) * 12 + 6 * (q % 2) + j if t < 72 else -1)
        for t in range(64):
            z, i, j = t // 18, t % 18 // 6, t % 6
            pack_b.append(z * 72 + (3 * (q // 2) + i) * 12 + 6 * (q % 2) + j if t < 54 else -1)
    for z in range(4):
        for i in range(6):
            for j in range(12):
                q = 2 * (1 - i // 3) + (1 - j // 6)
                open_a.append(80 * q + (z + 1) % 4 * 18 + i % 3 * 6 + j % 6)
                if z > 0:
                    open_b.append(64 * q + (z - 1) * 18 + i % 3 * 6 + j % 6)
    return one_hot(pack_a, 288), one_hot(open_a, 320), one_hot(pack_b, 288), one_hot(open_b, 256)


PLAN = {
    "start": ((0, 0), (4, 0), (1, 0)),
    "compact": (),
    "norm": ((0, 1), (1, 1), (2, 0), (4, 1), (0, 2), (1, 2), (2, 1), (3, 0), (0, 3), (4, 2), (0, 4)),
    "agg_scores": ((1, 3), (2, 2), (3, 1)),
    "agg_values": ((1, 4), (4, 3), (5, 0)),
    "agg_mix0": ((2, 3), (3, 2)),
    "agg_mix1": ((2, 4),),
    "b0_qkv": ((3, 3), (4, 4), (5, 1)),
    "b0_attention": ((3, 4),),
    "b0_proj": ((4, 5), (5, 2)),
    "b0_mlp1": ((5, 3),),
    "b0_mlp3": ((5, 4),),
}


def body(levels_in, surface, latents, level_codes, norm_gains, agg_query_w, agg_key_w, agg_value_w, agg_out_w,
         dec_query_w, dec_key_w, dec_value_w, dec_out_w, qkv_w, proj_w, mlp_in, mlp_out, regions):
    named = dict(agg_query_w=agg_query_w, agg_key_w=agg_key_w, agg_value_w=agg_value_w, agg_out_w=agg_out_w,
                 dec_query_w=dec_query_w, dec_key_w=dec_key_w, dec_value_w=dec_value_w, dec_out_w=dec_out_w,
                 qkv_w=qkv_w, proj_w=proj_w, mlp_in=mlp_in, mlp_out=mlp_out)
    vmem, smem = pl.BlockSpec(memory_space=pltpu.VMEM), pl.BlockSpec(memory_space=pltpu.SMEM)
    return pl.pallas_call(
        functools.partial(kernel, PLAN),
        out_shape=jax.ShapeDtypeStruct(levels_in.shape, BF16),
        in_specs=[vmem] * 5 + [smem] + [vmem] * 16,
        out_specs=vmem,
        scratch_shapes=[pltpu.VMEM(buffer_shape(chunk), BF16) for chunk in CHUNKS] + [
            pltpu.SemaphoreType.DMA((6, 18)),
            pltpu.SemaphoreType.DMA((6, 9)),
            pltpu.SemaphoreType.DMA((6, 8)),
            pltpu.SemaphoreType.DMA((2, 4)),
            pltpu.SemaphoreType.DMA((2, 3)),
            pltpu.VMEM((ROWS, D), F32),
            pltpu.VMEM((ROWS, D), BF16),
            pltpu.VMEM((ROWS, D), F32),
            pltpu.VMEM((ROWS, LATENT * HEADS), F32),
            pltpu.VMEM((D, LATENT * HEADS), BF16),
            pltpu.VMEM((D, LATENT * HEADS), BF16),
            pltpu.VMEM((D, LEVELS * HEADS), BF16),
            pltpu.VMEM((D, LEVELS * HEADS), BF16),
            pltpu.VMEM((TOKENS, D), F32),
            pltpu.VMEM((TOKENS, 3 * D), BF16),
            pltpu.VMEM((TOKENS, D), BF16),
            pltpu.VMEM((TOKENS, D), BF16),
            pltpu.VMEM((TOKENS, D), F32),
            pltpu.VMEM((2, WINDOW, WINDOW), F32),
            pltpu.VMEM((320, D), BF16),
            pltpu.VMEM((320, D), BF16),
            pltpu.VMEM((256, D), BF16),
            pltpu.VMEM((256, D), BF16),
            pltpu.VMEM((216, LEVELS * HEADS), F32),
        ],
        compiler_params=pltpu.CompilerParams(collective_id=0, has_side_effects=True, vmem_limit_bytes=58 * 2 ** 20),
        cost_estimate=pl.CostEstimate(flops=7 * 10 ** 9, bytes_accessed=10 ** 7, transcendentals=10 ** 7),
    )(levels_in, surface, latents, level_codes, norm_gains, regions, *[named[w] for w in WEIGHTS],
      *[jnp.asarray(m, BF16) for m in permutations()])


def solution(mesh):
    split_rows, split_middle = P("lat", None), P(None, "lat", None)
    in_specs = (P(None, "lat", "lon", None), P("lat", "lon", None), P(), P(), P()) + (split_rows,) * 8 + (
        split_middle,) * 4 + (P(None, "lat"),)
    return jax.shard_map(body, mesh=mesh, in_specs=in_specs, out_specs=P(None, "lat", "lon", None), check_vma=False)
```

time: 639 us -> 111 us (0.17)
  the two profiles are of different devices: /device:TPU:6 before, /device:TPU:1 now
where the time goes in v1:
time: 111 us
  Pallas kernels  105 us (95%)
  local copies, waits for them, and re-layouts  5.77 us (5%)
    pallas_call x1, Pallas kernels, body(): pl.pallas_call(functools.partial(kernel, PLAN), out_shape=jax.ShapeDtypeS...  105 us
    unnamed x1, local copies, waits for them, and re-layouts  2.89 us
    pallas_call x1, local copies, waits for them, and re-layouts, body(): pl.pallas_call(functools.partial(kernel, PLAN), out_shape=jax.ShapeDtypeS...  2.88 us

profile of v1, /device:TPU:1, one launch (start us, length us, event | category | flops | bytes accessed | tf_op | source)
XLA Modules:
  0.0 111.0 jit_solution(12950806714053254781)
XLA Ops:
  0.0 2.9 %copy.23.refs_0_ = bf16[13,6,12,512]{3,2,1,0:T(8,128)(2,1)} copy(bf16[13,6,12,512]{3,0,2,1:T(8,128)(2,1)} %param.22) | data formatting | bytes 1916928 | tf_op args[0]
  2.9 105.2 %shard_map.208 = bf16[13,6,12,512]{3,2,1,0:T(8,128)(2,1)} custom-call(bf16[13,6,12,512]{3,2,1,0:T(8,128)(2,1)} %copy.23.refs_0_, bf16[6,12,512]{2,1,0:T(8,128)(2,1)} %refs_1_.1, bf16[3,512]{1,0:T(4,128)(2,1)} %refs_2_.1, bf16[13,512]{1,0:T(8,128)(2,1)} %refs_3_.1, f32[6,512]{1,0:T(8,128)} %refs_4_.1, s32[4,6]{1,0:T(4,128)} %refs_5_.1, ...), custom_call_target="tpu_custom_call" | custom-call | flops 7000000000 | bytes 10000000 | tf_op jit(solution)/shard_map/pallas_call | solution.py:524
  108.1 2.9 %copy.24 = bf16[13,6,12,512]{3,0,2,1:T(8,128)(2,1)} copy(bf16[13,6,12,512]{3,2,1,0:T(8,128)(2,1)} %shard_map.208) | data formatting | bytes 1916928 | tf_op jit(solution)/shard_map/pallas_call | solution.py:524

commit v2 on v1

--- a/solution.py
+++ b/solution.py
@@ -269,36 +269,28 @@
     return pl.ds(pl.multiple_of(index * size, size & -size), size)
 
 
-def norm_rows(src, dst, gain, rows, block=48):
+def norm_rows(load, dst, gain, rows, block=48):
     def step(n, _):
-        dst[rows_of(n, block)] = normed(src[rows_of(n, block)], gain)
+        dst[rows_of(n, block)] = normed(load(rows_of(n, block)), gain)
         return 0
     lax.fori_loop(0, rows // block, step, 0, unroll=True)
 
 
-def attention(packed, attended, masks):
+def attention(packed, attended, mask, w):
     lane = lane_head((WINDOW, 128))
     ones = jnp.ones((WINDOW, 128), BF16)
-
-    def step(n, _):
-        w, g = lax.div(n, 4), lax.rem(n, 4)
-        rows = rows_of(w, WINDOW)
-        q, k, v = (packed[rows, pl.ds(pl.multiple_of(g * 128 + part * D, 128), 128)] for part in range(3))
-        heads = [jnp.where(lane == m, q, jnp.zeros_like(q)) for m in range(4)]
-        weights = []
-        for m in range(4):
-            e = jnp.exp(dot_t(heads[m], k) * SCALE)
-            if masks is not None:
-                e = e * masks[w]
-            weights.append(e.astype(BF16))
+    rows = slice(WINDOW * w, WINDOW * w + WINDOW)
+    for g in range(4):
+        q, k, v = (packed[rows, 128 * g + part * D:128 * g + part * D + 128] for part in range(3))
         both = jnp.concatenate([v, ones], axis=1)
         total = jnp.zeros((WINDOW, 128), F32)
         for m in range(4):
-            mixed = dot(weights[m], both)
+            e = jnp.exp(dot_t(jnp.where(lane == m, q, jnp.zeros_like(q)), k) * SCALE)
+            if mask is not None:
+                e = e * mask
+            mixed = dot(e.astype(BF16), both)
             total = jnp.where(lane == m, mixed[:, :128] / mixed[:, 128:], total)
-        attended[rows, pl.ds(pl.multiple_of(g * 128, 128), 128)] = total.astype(BF16)
-        return 0
-    lax.fori_loop(0, 8, step, 0)
+        attended[rows, 128 * g:128 * g + 128] = total.astype(BF16)
 
 
 def kernel(plan, *refs):
@@ -307,7 +299,7 @@
     (pack1, open1, pack2, open2), refs = refs[:4], refs[4:]
     out_ref, refs = refs[0], refs[1:]
     buffers, refs = refs[:len(CHUNKS)], refs[len(CHUNKS):]
-    (send, recv, core_recv, halo_send, halo_recv, stage, norm, values, expo, fa_high, fa_low, fd_high, fd_low,
+    (send, recv, core_recv, halo_send, halo_recv, tiled, norm, values, expo, fa_high, fa_low, fd_high, fd_low,
      grid, packed, attended, grid_norm, total, masks, out1, in1, out2, in2, dec_expo) = refs
 
     place = Place()
@@ -319,7 +311,6 @@
     friends += [place.beside(i, j) for i, j in ((1, 0), (0, 1), (1, 1), (-1, 0), (0, -1), (-1, -1))]
     for friend in friends:
         pl.semaphore_signal(barrier, inc=1, device_id=friend, device_id_type=pl.DeviceIdType.MESH)
-    pl.semaphore_wait(barrier, len(friends))
 
     carriers, count = [], [0, 0]
     for chunk, buf in zip(CHUNKS, buffers):
@@ -341,15 +332,16 @@
         for n in numbers:
             carriers[n].arrived()
 
-    pump("start")
-    stage[936:960] = jnp.zeros((24, D), F32)
-    for level in range(LEVELS):
-        for i in range(6):
-            stage[PATCHES * level + 12 * i:PATCHES * level + 12 * i + 12] = levels_ref[level, i].astype(F32)
+    tiled[:, 936:960] = jnp.zeros((4, 24, 128), F32)
+    for n in range(PATCHES):
+        rows = levels_ref[n // 12, n % 12].astype(F32)
+        for c in range(4):
+            tiled[c, pl.ds(n, LEVELS, stride=PATCHES)] = rows[:, 128 * c:128 * c + 128]
     for i in range(6):
         grid[12 * i:12 * i + 12] = surface_ref[i].astype(F32)
-    pump("compact")
-    norm_rows(stage, norm, gains_ref[0:1], ROWS)
+    norm_rows(lambda rows: jnp.concatenate([tiled[c, rows] for c in range(4)], axis=1), norm, gains_ref[0:1], ROWS)
+    pl.semaphore_wait(barrier, len(friends))
+    pump("start")
     pump("norm")
     ready(0)
     score_matrix(latents_ref[...], LATENT, weight(0, 0), weight(0, 1), fa_high, fa_low)
@@ -368,16 +360,14 @@
         return 0
     lax.fori_loop(0, ROWS // 192, value_step, 0)
     pump("agg_values")
-    inverse = 1.0 / lax.fori_loop(
-        0, LEVELS, lambda n, s: s + expo[rows_of(n, PATCHES)], jnp.zeros((PATCHES, LATENT * HEADS), F32))
+    level_rows = [slice(PATCHES * n, PATCHES * n + PATCHES) for n in range(LEVELS)]
+    inverse = 1.0 / sum(expo[rows] for rows in level_rows)
+    probs = jnp.concatenate([expo[rows] * inverse for rows in level_rows], axis=0).astype(BF16)
     for a in range(LATENT):
         spread = spread_matrix(LATENT * HEADS, HEADS * a)
-
-        def mix_step(n, s):
-            probs = (expo[rows_of(n, PATCHES)] * inverse).astype(BF16)
-            return s + dot(probs, spread) * values[rows_of(n, PATCHES)]
-        mixed = lax.fori_loop(0, LEVELS, mix_step, jnp.zeros((PATCHES, D), F32))
-        total[PATCHES * a:PATCHES * a + PATCHES] = mixed
+        for cols in (slice(0, 256), slice(256, 512)):
+            wide = dot(probs, spread[:, cols])
+            total[PATCHES * a:PATCHES * a + PATCHES, cols] = sum(wide[rows] * values[rows, cols] for rows in level_rows)
         pump("agg_mix%d" % a)
     projected = dot(total[0:216].astype(BF16), weight(1, 1))
     for a in range(LATENT):
@@ -387,7 +377,7 @@
 
     def block(b):
         name = "b%d_" % b
-        norm_rows(grid, grid_norm, gains_ref[2 + 2 * b:3 + 2 * b], TOKENS)
+        norm_rows(lambda rows: grid[rows], grid_norm, gains_ref[2 + 2 * b:3 + 2 * b], TOKENS)
         qkv_n, proj_n = (7, 6) if b else (2, 3)
         in_n, out_n = (8, 9) if b else (4, 5)
         ready(qkv_n)
@@ -395,21 +385,20 @@
             cols = buffers[qkv_n][0, :, :, :, :, 256 * n:256 * n + 256].reshape(D, 256)
             packed[:, 256 * n:256 * n + 256] = dot(grid_norm[...], cols).astype(BF16)
         pump(name + "qkv")
-        attention(packed, attended, masks if b else None)
-        pump(name + "attention")
+        for w in range(2):
+            attention(packed, attended, masks[w] if b else None, w)
+            pump(name + "attention%d" % w)
         ready(proj_n)
         grid[...] = rounded(grid[...] + dot(attended[...], weight(proj_n)))
         pump(name + "proj")
-        norm_rows(grid, grid_norm, gains_ref[3 + 2 * b:4 + 2 * b], TOKENS)
+        norm_rows(lambda rows: grid[rows], grid_norm, gains_ref[3 + 2 * b:4 + 2 * b], TOKENS)
         ready(in_n, out_n)
         total[...] = grid[...]
 
-        def step(n, _):
-            hidden = gelu(dot_t(grid_norm[...], buffers[in_n][0, n].reshape(256, D)))
-            total[...] += dot(hidden, buffers[out_n][0, n].reshape(256, D))
-            return 0
         for part in range(4):
-            lax.fori_loop(2 * part, 2 * part + 2, step, 0)
+            hidden = [gelu(dot_t(grid_norm[...], buffers[in_n][0, n].reshape(256, D)))
+                      for n in (2 * part, 2 * part + 1)]
+            total[...] += sum(dot(hidden[n], buffers[out_n][0, 2 * part + n].reshape(256, D)) for n in range(2))
             pump(name + "mlp%d" % part)
 
     block(0)
@@ -456,22 +445,22 @@
     ready(11)
     total[0:216] = dot(atmos, weight(11, 0))
 
-    def decode_step(n, _):
-        spread = spread_matrix(LEVELS * HEADS, HEADS * n)
-        wide = dot(dec_expo[...].astype(BF16), spread) * total[0:216]
-        stage[rows_of(n, PATCHES)] = wide[:PATCHES] + wide[PATCHES:2 * PATCHES] + wide[2 * PATCHES:]
-        return 0
-    lax.fori_loop(0, LEVELS, decode_step, 0)
+    spread = spread_matrix(HEADS, 0)
+    for n in range(LEVELS):
+        wide = dot(dec_expo[:, HEADS * n:HEADS * n + HEADS].astype(BF16), spread) * total[0:216]
+        values[PATCHES * n:PATCHES * n + PATCHES] = (
+            wide[:PATCHES] + wide[PATCHES:2 * PATCHES] + wide[2 * PATCHES:])
 
     def out_step(n, _):
-        values[rows_of(n, 192)] = dot(stage[rows_of(n, 192)].astype(BF16), weight(11, 1))
+        rows = dot(values[rows_of(n, 192)].astype(BF16), weight(11, 1))
+        for c in range(4):
+            tiled[c, rows_of(n, 192)] = rows[:, 128 * c:128 * c + 128]
         return 0
     lax.fori_loop(0, ROWS // 192, out_step, 0)
-    for level in range(LEVELS):
-        code = codes_ref[level:level + 1].astype(F32)
-        for i in range(6):
-            rows = values[PATCHES * level + 12 * i:PATCHES * level + 12 * i + 12]
-            out_ref[level, i] = (code + rows).astype(BF16)
+    codes = codes_ref[...].astype(F32)
+    for n in range(PATCHES):
+        rows = jnp.concatenate([tiled[c, pl.ds(n, LEVELS, stride=PATCHES)] for c in range(4)], axis=1)
+        out_ref[n // 12, n % 12] = (codes + rows).astype(BF16)
     for carrier in carriers:
         carrier.finish()
 
@@ -500,18 +489,18 @@
 
 
 PLAN = {
-    "start": ((0, 0), (4, 0), (1, 0)),
-    "compact": (),
-    "norm": ((0, 1), (1, 1), (2, 0), (4, 1), (0, 2), (1, 2), (2, 1), (3, 0), (0, 3), (4, 2), (0, 4)),
-    "agg_scores": ((1, 3), (2, 2), (3, 1)),
-    "agg_values": ((1, 4), (4, 3), (5, 0)),
-    "agg_mix0": ((2, 3), (3, 2)),
-    "agg_mix1": ((2, 4),),
-    "b0_qkv": ((3, 3), (4, 4), (5, 1)),
-    "b0_attention": ((3, 4),),
-    "b0_proj": ((4, 5), (5, 2)),
-    "b0_mlp1": ((5, 3),),
-    "b0_mlp3": ((5, 4),),
+    "start": ((0, 0), (4, 0)),
+    "norm": ((1, 0), (4, 1), (0, 1), (1, 1), (0, 2), (2, 0), (1, 2), (5, 0), (0, 3), (2, 1), (4, 2),
+             (1, 3), (0, 4), (3, 0), (4, 3), (2, 2)),
+    "agg_mix0": ((3, 1),),
+    "agg_mix2": ((1, 4), (2, 3), (4, 4), (3, 2)),
+    "b0_qkv": ((4, 5),),
+    "b0_attention0": ((2, 4), (5, 1)),
+    "b0_proj": ((3, 3),),
+    "b0_mlp1": ((5, 2),),
+    "b0_mlp3": ((3, 4),),
+    "b1_qkv": ((5, 3),),
+    "b1_mlp3": ((5, 4),),
 }
 
 
@@ -521,9 +510,9 @@
                  dec_query_w=dec_query_w, dec_key_w=dec_key_w, dec_value_w=dec_value_w, dec_out_w=dec_out_w,
                  qkv_w=qkv_w, proj_w=proj_w, mlp_in=mlp_in, mlp_out=mlp_out)
     vmem, smem = pl.BlockSpec(memory_space=pltpu.VMEM), pl.BlockSpec(memory_space=pltpu.SMEM)
-    return pl.pallas_call(
+    decoded = pl.pallas_call(
         functools.partial(kernel, PLAN),
-        out_shape=jax.ShapeDtypeStruct(levels_in.shape, BF16),
+        out_shape=jax.ShapeDtypeStruct((6, 12, LEVELS, D), BF16),
         in_specs=[vmem] * 5 + [smem] + [vmem] * 16,
         out_specs=vmem,
         scratch_shapes=[pltpu.VMEM(buffer_shape(chunk), BF16) for chunk in CHUNKS] + [
@@ -532,7 +521,7 @@
             pltpu.SemaphoreType.DMA((6, 8)),
             pltpu.SemaphoreType.DMA((2, 4)),
             pltpu.SemaphoreType.DMA((2, 3)),
-            pltpu.VMEM((ROWS, D), F32),
+            pltpu.VMEM((4, ROWS, 128), F32),
             pltpu.VMEM((ROWS, D), BF16),
             pltpu.VMEM((ROWS, D), F32),
             pltpu.VMEM((ROWS, LATENT * HEADS), F32),
@@ -554,8 +543,9 @@
         ],
         compiler_params=pltpu.CompilerParams(collective_id=0, has_side_effects=True, vmem_limit_bytes=58 * 2 ** 20),
         cost_estimate=pl.CostEstimate(flops=7 * 10 ** 9, bytes_accessed=10 ** 7, transcendentals=10 ** 7),
-    )(levels_in, surface, latents, level_codes, norm_gains, regions, *[named[w] for w in WEIGHTS],
+    )(jnp.transpose(levels_in, (1, 2, 0, 3)), surface, latents, level_codes, norm_gains, regions, *[named[w] for w in WEIGHTS],
       *[jnp.asarray(m, BF16) for m in permutations()])
+    return jnp.transpose(decoded, (2, 0, 1, 3))
 
 
 def solution(mesh):

time: 111 us -> 90.1 us (0.81)
  Pallas kernels: 105 us -> 87.5 us
  local copies, waits for them, and re-layouts: 5.77 us -> 2.42 us
    pallas_call x1, Pallas kernels: 105 us -> 87.5 us  [body(): pl.pallas_call(functools.partial(kernel, PLAN), out_shape=jax.ShapeDtypeS...]
    pallas_call x1 -> x0, local copies, waits for them, and re-layouts: 2.88 us -> none  [body(): pl.pallas_call(functools.partial(kernel, PLAN), out_shape=jax.ShapeDtypeS...]
where the time goes in v2:
time: 90.1 us; the launch traced here: 89.9 us
  Pallas kernels  87.5 us (97%)
  local copies, waits for them, and re-layouts  2.42 us (3%)
    pallas_call x1, Pallas kernels, body(): pl.pallas_call(functools.partial(kernel, PLAN), out_shape=jax.ShapeDtypeS...  87.5 us
    unnamed x1, local copies, waits for them, and re-layouts  2.42 us

profile of v2, /device:TPU:1, one launch (start us, length us, event | category | flops | bytes accessed | tf_op | source)
XLA Modules:
  0.0 89.9 jit_solution(18050164221941214466)
XLA Ops:
  0.0 87.5 %shard_map.208 = bf16[6,12,13,512]{3,2,1,0:T(8,128)(2,1)} custom-call(bf16[6,12,13,512]{3,2,1,0:T(8,128)(2,1)} %bitcast.3, bf16[6,12,512]{2,1,0:T(8,128)(2,1)} %refs_1_.1, bf16[3,512]{1,0:T(4,128)(2,1)} %refs_2_.1, bf16[13,512]{1,0:T(8,128)(2,1)} %refs_3_.1, f32[6,512]{1,0:T(8,128)} %refs_4_.1, s32[4,6]{1,0:T(4,128)} %refs_5_.1, bf16[32,512]{1,0:T(8,128)(2,1)} %refs_6_.1, ...), custom_call_target="tpu_custom_call" | custom-call | flops 7000000000 | bytes 10000000 | tf_op jit(solution)/shard_map/pallas_call | solution.py:513
  87.5 2.4 %copy.24 = bf16[13,6,12,512]{3,0,2,1:T(8,128)(2,1)} copy(bf16[13,6,12,512]{3,0,2,1:T(8,128)(2,1)} %bitcast.2) | data formatting | bytes 1916928

commit v3 on v2

--- a/solution.py
+++ b/solution.py
@@ -23,16 +23,16 @@
 BF16 = jnp.bfloat16
 
 CHUNKS = (
-    ((("agg_query_w", None), ("agg_key_w", None)), 32, 512, 0, "xy"),
-    ((("agg_value_w", None), ("agg_out_w", None)), 32, 512, 1, "yx"),
+    ((("agg_query_w", None), ("agg_key_w", None)), 32, 512, 0, "xyu"),
+    ((("agg_value_w", None), ("agg_out_w", None)), 32, 512, 1, "yxu"),
     ((("qkv_w", 0),), 32, 1536, 0, "xy"),
     ((("proj_w", 0),), 32, 512, 1, "yx"),
-    ((("mlp_in", 0),), 128, 512, 0, "xy"),
-    ((("mlp_out", 0),), 128, 512, 1, "yx"),
+    ((("mlp_in", 0),), 128, 512, 0, "z"),
+    ((("mlp_out", 0),), 128, 512, 1, "z"),
     ((("proj_w", 1),), 32, 512, 0, "xy"),
     ((("qkv_w", 1),), 32, 1536, 1, "yx"),
-    ((("mlp_in", 1),), 128, 512, 0, "z"),
-    ((("mlp_out", 1),), 128, 512, 1, "z"),
+    ((("mlp_in", 1),), 128, 512, 0, "xy"),
+    ((("mlp_out", 1),), 128, 512, 1, "yx"),
     ((("dec_query_w", None), ("dec_key_w", None)), 32, 512, 0, "xy"),
     ((("dec_value_w", None), ("dec_out_w", None)), 32, 512, 1, "yx"),
 )
@@ -82,7 +82,7 @@
         self.place, self.chunk, self.sources, self.buf, self.index = place, chunk, sources, buf, index
         self.send, self.recv, self.core_recv = send, recv, core_recv
         self.core, self.kind = chunk[3], chunk[4]
-        self.last = 5 if self.kind == "z" else 4
+        self.last = 5 if self.kind == "z" else 3 if self.kind.endswith("u") else 4
         self.done = 0
 
     def cols(self, y):
@@ -90,7 +90,7 @@
         return pl.ds(pl.multiple_of(y * width, 128), width)
 
     def part(self, stage, c, zs=ALL):
-        d1, d2 = self.kind
+        d1, d2 = self.kind[:2]
         at = {d2: c}
         if stage == 1:
             at = {d1: c, d2: getattr(self.place, d2)}
@@ -150,19 +150,24 @@
                 found.append(((slab, 2 * task - 3 + n), self.to(onward, 2 * task - 1 + n, z=p.turn("z", sign))))
                 found.append((None, self.to_core(slab, 2 * task - 3 + n)))
             return found
-        d1, d2 = self.kind
+        d1, d2 = self.kind[:2]
         if task == 1:
             own = self.part(1, getattr(p, d1))
             return [(None, self.to(own, 1, **{d1: p.turn(d1, 1)})), (None, self.to(own, 2, **{d1: p.turn(d1, -1)})),
                     (None, self.to(own, 3, **{d1: p.turn(d1, 2)}))]
         up, down, far = p.turn(d2, 1), p.turn(d2, -1), p.turn(d2, 2)
         low, high = pl.ds(0, 4), pl.ds(4, 4)
+        direct = self.kind.endswith("u")
         if task == 2:
             own = self.part(2, getattr(p, d2))
+            more = [(None, self.to(own, 7, **{d2: far}))] if direct else []
             return [((self.part(1, p.turn(d1, -1)), 1), None), ((self.part(1, p.turn(d1, 1)), 2), None),
                     ((self.part(1, p.turn(d1, 2)), 3), None),
                     (None, self.to(own, 5, **{d2: up})), (None, self.to(own, 6, **{d2: down})),
-                    (None, self.to_core(own, 0))]
+                    (None, self.to_core(own, 0))] + more
+        if task == 3 and direct:
+            return [((self.part(2, c), 5 + k), self.to_core(self.part(2, c), 1 + k))
+                    for k, c in enumerate((down, up, far))]
         if task == 3:
             return [((self.part(2, down), 5), self.to(self.part(2, down, low), 7, **{d2: up})),
                     ((self.part(2, up), 6), self.to(self.part(2, up, high), 8, **{d2: down})),
@@ -294,15 +299,21 @@
 
 
 def kernel(plan, *refs):
-    (levels_ref, surface_ref, latents_ref, codes_ref, gains_ref, regions_ref), refs = refs[:6], refs[6:]
+    (latents_ref, codes_ref, gains_ref, regions_ref), refs = refs[:4], refs[4:]
     sources, refs = dict(zip(WEIGHTS, refs[:12])), refs[12:]
-    (pack1, open1, pack2, open2), refs = refs[:4], refs[4:]
+    far, refs = refs[:8], refs[8:]
     out_ref, refs = refs[0], refs[1:]
+    near, refs = refs[:8], refs[8:]
+    levels_ref, surface_ref, pack1a, pack1b, open1, pack2a, pack2b, open2 = near
     buffers, refs = refs[:len(CHUNKS)], refs[len(CHUNKS):]
     (send, recv, core_recv, halo_send, halo_recv, tiled, norm, values, expo, fa_high, fa_low, fd_high, fd_low,
-     grid, packed, attended, grid_norm, total, masks, out1, in1, out2, in2, dec_expo) = refs
+     grid, packed, attended, grid_norm, total, hidden, masks, out1, in1, out2, in2, dec_expo, result,
+     near_sem, out_sem) = refs
 
     place = Place()
+    loads = [pltpu.make_async_copy(src, dst, near_sem.at[n]) for n, (src, dst) in enumerate(zip(far, near))]
+    for load in loads:
+        load.start()
     barrier = pltpu.get_barrier_semaphore()
     friends = [place.device(z=place.turn("z", n)) for n in range(1, 8)]
     friends += [place.device(x=place.turn("x", n)) for n in range(1, 4)]
@@ -311,7 +322,7 @@
     friends += [place.beside(i, j) for i, j in ((1, 0), (0, 1), (1, 1), (-1, 0), (0, -1), (-1, -1))]
     for friend in friends:
         pl.semaphore_signal(barrier, inc=1, device_id=friend, device_id_type=pl.DeviceIdType.MESH)
-
+    pl.semaphore_wait(barrier, len(friends))
     carriers, count = [], [0, 0]
     for chunk, buf in zip(CHUNKS, buffers):
         own = [sources[w] if k is None else sources[w].at[k] for w, k in chunk[0]]
@@ -332,16 +343,18 @@
         for n in numbers:
             carriers[n].arrived()
 
+    pump("start")
     tiled[:, 936:960] = jnp.zeros((4, 24, 128), F32)
+    loads[0].wait()
+    loads[1].wait()
     for n in range(PATCHES):
         rows = levels_ref[n // 12, n % 12].astype(F32)
         for c in range(4):
             tiled[c, pl.ds(n, LEVELS, stride=PATCHES)] = rows[:, 128 * c:128 * c + 128]
     for i in range(6):
         grid[12 * i:12 * i + 12] = surface_ref[i].astype(F32)
+    pump("compact")
     norm_rows(lambda rows: jnp.concatenate([tiled[c, rows] for c in range(4)], axis=1), norm, gains_ref[0:1], ROWS)
-    pl.semaphore_wait(barrier, len(friends))
-    pump("start")
     pump("norm")
     ready(0)
     score_matrix(latents_ref[...], LATENT, weight(0, 0), weight(0, 1), fa_high, fa_low)
@@ -375,7 +388,7 @@
         grid[PATCHES * (a + 1):PATCHES * (a + 2)] = rounded(latents_ref[a:a + 1].astype(F32) + rows)
     pump("agg_out")
 
-    def block(b):
+    def block(b, done):
         name = "b%d_" % b
         norm_rows(lambda rows: grid[rows], grid_norm, gains_ref[2 + 2 * b:3 + 2 * b], TOKENS)
         qkv_n, proj_n = (7, 6) if b else (2, 3)
@@ -392,29 +405,46 @@
         grid[...] = rounded(grid[...] + dot(attended[...], weight(proj_n)))
         pump(name + "proj")
         norm_rows(lambda rows: grid[rows], grid_norm, gains_ref[3 + 2 * b:4 + 2 * b], TOKENS)
-        ready(in_n, out_n)
-        total[...] = grid[...]
-
+        ready(in_n)
         for part in range(4):
-            hidden = [gelu(dot_t(grid_norm[...], buffers[in_n][0, n].reshape(256, D)))
-                      for n in (2 * part, 2 * part + 1)]
-            total[...] += sum(dot(hidden[n], buffers[out_n][0, 2 * part + n].reshape(256, D)) for n in range(2))
+            cols = slice(512 * part, 512 * part + 512)
+            hidden[:, cols] = gelu(dot_t(grid_norm[...], buffers[in_n][0, 2 * part:2 * part + 2].reshape(512, D)))
             pump(name + "mlp%d" % part)
-
-    block(0)
-
-    def exchange(source, target, size, slot, own, sends):
-        keep = pltpu.make_async_copy(source.at[pl.ds(own * size, size)], target.at[pl.ds(own * size, size)],
-                                     halo_send.at[slot, 3])
-        copies = [remote(source.at[pl.ds(q * size, size)], target.at[pl.ds(q * size, size)], halo_send.at[slot, n],
-                         halo_recv.at[slot, n], place.beside(i, j)) for n, (q, i, j) in enumerate(sends)]
+        ready(out_n)
+        for w in range(2):
+            rows = slice(WINDOW * w, WINDOW * w + WINDOW)
+            total[rows] = grid[rows] + dot(hidden[rows], weight(out_n))
+            done(w)
+            pump(name + "half%d" % w)
+
+    def exchange(source, target, first, size, slot, own, sends):
+        at = [pl.ds(first + q * size, size) for q in range(4)]
+        copies = [remote(source.at[at[q]], target.at[at[q]], halo_send.at[slot, n], halo_recv.at[slot, n],
+                         place.beside(i, j)) for n, (q, i, j) in enumerate(sends)]
+        copies.append(pltpu.make_async_copy(source.at[at[own]], target.at[at[own]], halo_send.at[slot, 3]))
         for copy in copies:
             copy.start()
-        keep.start()
-        return copies, keep
-
-    out1[...] = dot(pack1[...], total[...].astype(BF16)).astype(BF16)
-    copies, keep = exchange(out1, in1, 80, 0, 3, ((1, -1, 0), (2, 0, -1), (0, -1, -1)))
+        moving.extend(copies)
+
+    moving = []
+    for load in loads[2:]:
+        load.wait()
+
+    def first_half_windows(w):
+        rows = slice(WINDOW * w, WINDOW * w + WINDOW)
+        out1[192 * w:192 * w + 192] = dot((pack1a, pack1b)[w][...], total[rows].astype(BF16)).astype(BF16)
+        exchange(out1, in1, 192 * w, 48, w, 3, ((0, -1, -1), (1, -1, 0), (2, 0, -1)))
+
+    def last_half_windows(w):
+        size, rows = (48, 32)[w], slice(WINDOW * w, WINDOW * w + WINDOW)
+        out2[192 * w:192 * w + 4 * size] = dot((pack2a, pack2b)[w][...], total[rows].astype(BF16)).astype(BF16)
+        exchange(out2, in2, 192 * w, size, 2 + w, 0, ((3, 1, 1), (2, 1, 0), (1, 0, 1)))
+
+    def arrive():
+        while moving:
+            moving.pop(0).wait()
+
+    block(0, first_half_windows)
     pump("halo1")
     ids = [[regions_ref[level, i] for i in range(6)] for level in range(4)]
     for w in range(2):
@@ -425,19 +455,13 @@
             rows_id = jnp.where(lax.broadcasted_iota(jnp.int32, (WINDOW, WINDOW), 0) >= 12 * n, value, rows_id)
             cols_id = jnp.where(lax.broadcasted_iota(jnp.int32, (WINDOW, WINDOW), 1) >= 12 * n, value, cols_id)
         masks[w] = jnp.where(rows_id == cols_id, 1.0, 0.0)
-    for copy in copies:
-        copy.wait()
-    keep.wait()
+    arrive()
     grid[...] = dot(open1[...], in1[...])
-    block(1)
-    out2[...] = dot(pack2[...], total[...].astype(BF16)).astype(BF16)
-    copies, keep = exchange(out2, in2, 64, 1, 0, ((2, 1, 0), (1, 0, 1), (3, 1, 1)))
+    block(1, last_half_windows)
     pump("halo2")
     ready(10)
     score_matrix(codes_ref[...], LEVELS, weight(10, 0), weight(10, 1), fd_high, fd_low)
-    for copy in copies:
-        copy.wait()
-    keep.wait()
+    arrive()
     atmos = normed(dot(open2[...], in2[...]), gains_ref[1:2])
     expos = jnp.exp((dot(atmos, fd_high[...]) + dot(atmos, fd_low[...])) * SCALE)
     inverse = 1.0 / (expos[:PATCHES] + expos[PATCHES:2 * PATCHES] + expos[2 * PATCHES:])
@@ -458,9 +482,14 @@
         return 0
     lax.fori_loop(0, ROWS // 192, out_step, 0)
     codes = codes_ref[...].astype(F32)
+    stores = [pltpu.make_async_copy(result.at[i], out_ref.at[i], out_sem.at[i]) for i in range(6)]
     for n in range(PATCHES):
         rows = jnp.concatenate([tiled[c, pl.ds(n, LEVELS, stride=PATCHES)] for c in range(4)], axis=1)
-        out_ref[n // 12, n % 12] = (codes + rows).astype(BF16)
+        result[n // 12, n % 12] = (codes + rows).astype(BF16)
+        if n % 12 == 11:
+            stores[n // 12].start()
+    for store in stores:
+        store.wait()
     for carrier in carriers:
         carrier.finish()
 
@@ -470,37 +499,39 @@
 
 
 def permutations():
-    pack_a, open_a, pack_b, open_b = [], [], [], []
-    for q in range(4):
-        for t in range(80):
-            z, i, j = t // 18, t % 18 // 6, t % 6
-            pack_a.append(z * 72 + (3 * (q // 2) + i) * 12 + 6 * (q % 2) + j if t < 72 else -1)
-        for t in range(64):
-            z, i, j = t // 18, t % 18 // 6, t % 6
-            pack_b.append(z * 72 + (3 * (q // 2) + i) * 12 + 6 * (q % 2) + j if t < 54 else -1)
+    def quarter(q, z, i, j):
+        return (z * 6 + 3 * (q // 2) + i) * 12 + 6 * (q % 2) + j
+
+    def pack(levels, size):
+        picked = []
+        for q in range(4):
+            rows = [quarter(q, z, i, j) for z in range(levels) for i in range(3) for j in range(6)]
+            picked += rows + [-1] * (size - len(rows))
+        return one_hot(picked, WINDOW)
+
+    open_a, open_b = [], []
     for z in range(4):
         for i in range(6):
             for j in range(12):
-                q = 2 * (1 - i // 3) + (1 - j // 6)
-                open_a.append(80 * q + (z + 1) % 4 * 18 + i % 3 * 6 + j % 6)
+                q, at = 2 * (1 - i // 3) + (1 - j // 6), i % 3 * 6 + j % 6
+                level = (z + 1) % 4
+                open_a.append(192 * (level // 2) + 48 * q + 18 * (level % 2) + at)
                 if z > 0:
-                    open_b.append(64 * q + (z - 1) * 18 + i % 3 * 6 + j % 6)
-    return one_hot(pack_a, 288), one_hot(open_a, 320), one_hot(pack_b, 288), one_hot(open_b, 256)
+                    open_b.append(192 + 32 * q + at if z == 3 else 48 * q + 18 * (z - 1) + at)
+    return pack(2, 48), pack(2, 48), one_hot(open_a, 384), pack(2, 48), pack(1, 32), one_hot(open_b, 320)
 
 
 PLAN = {
-    "start": ((0, 0), (4, 0)),
-    "norm": ((1, 0), (4, 1), (0, 1), (1, 1), (0, 2), (2, 0), (1, 2), (5, 0), (0, 3), (2, 1), (4, 2),
-             (1, 3), (0, 4), (3, 0), (4, 3), (2, 2)),
-    "agg_mix0": ((3, 1),),
-    "agg_mix2": ((1, 4), (2, 3), (4, 4), (3, 2)),
-    "b0_qkv": ((4, 5),),
-    "b0_attention0": ((2, 4), (5, 1)),
-    "b0_proj": ((3, 3),),
-    "b0_mlp1": ((5, 2),),
-    "b0_mlp3": ((3, 4),),
-    "b1_qkv": ((5, 3),),
-    "b1_mlp3": ((5, 4),),
+    "start": ((0, 0), (3, 0), (1, 0), (2, 0), (2, 1), (0, 1), (3, 1), (1, 1), (0, 2), (4, 0), (5, 0), (2, 2), (1, 2), (4, 1),),
+    "compact": ((0, 3),),
+    "norm": ((3, 2), (2, 3), (1, 3), (4, 2),),
+    "agg_mix0": ((2, 4), (3, 3),),
+    "agg_mix2": ((1, 4),),
+    "agg_out": ((5, 1),),
+    "b0_attention1": ((2, 5), (4, 3),),
+    "halo1": ((5, 2), (3, 4), (4, 4),),
+    "b1_attention1": ((5, 3),),
+    "halo2": ((5, 4),),
 }
 
 
@@ -510,17 +541,20 @@
                  dec_query_w=dec_query_w, dec_key_w=dec_key_w, dec_value_w=dec_value_w, dec_out_w=dec_out_w,
                  qkv_w=qkv_w, proj_w=proj_w, mlp_in=mlp_in, mlp_out=mlp_out)
     vmem, smem = pl.BlockSpec(memory_space=pltpu.VMEM), pl.BlockSpec(memory_space=pltpu.SMEM)
+    far = pl.BlockSpec(memory_space=pl.ANY)
+    loaded = [jnp.transpose(levels_in, (1, 2, 0, 3)), surface] + [jnp.asarray(m, BF16) for m in permutations()]
     decoded = pl.pallas_call(
         functools.partial(kernel, PLAN),
         out_shape=jax.ShapeDtypeStruct((6, 12, LEVELS, D), BF16),
-        in_specs=[vmem] * 5 + [smem] + [vmem] * 16,
-        out_specs=vmem,
-        scratch_shapes=[pltpu.VMEM(buffer_shape(chunk), BF16) for chunk in CHUNKS] + [
+        in_specs=[vmem] * 3 + [smem] + [far] * 20,
+        out_specs=far,
+        scratch_shapes=[pltpu.VMEM(a.shape, BF16) for a in loaded] + [
+            pltpu.VMEM(buffer_shape(chunk), BF16) for chunk in CHUNKS] + [
             pltpu.SemaphoreType.DMA((6, 18)),
             pltpu.SemaphoreType.DMA((6, 9)),
             pltpu.SemaphoreType.DMA((6, 8)),
-            pltpu.SemaphoreType.DMA((2, 4)),
-            pltpu.SemaphoreType.DMA((2, 3)),
+            pltpu.SemaphoreType.DMA((4, 4)),
+            pltpu.SemaphoreType.DMA((4, 3)),
             pltpu.VMEM((4, ROWS, 128), F32),
             pltpu.VMEM((ROWS, D), BF16),
             pltpu.VMEM((ROWS, D), F32),
@@ -534,17 +568,20 @@
             pltpu.VMEM((TOKENS, D), BF16),
             pltpu.VMEM((TOKENS, D), BF16),
             pltpu.VMEM((TOKENS, D), F32),
+            pltpu.VMEM((TOKENS, 4 * D), BF16),
             pltpu.VMEM((2, WINDOW, WINDOW), F32),
+            pltpu.VMEM((384, D), BF16),
+            pltpu.VMEM((384, D), BF16),
             pltpu.VMEM((320, D), BF16),
             pltpu.VMEM((320, D), BF16),
-            pltpu.VMEM((256, D), BF16),
-            pltpu.VMEM((256, D), BF16),
             pltpu.VMEM((216, LEVELS * HEADS), F32),
+            pltpu.VMEM((6, 12, LEVELS, D), BF16),
+            pltpu.SemaphoreType.DMA((8,)),
+            pltpu.SemaphoreType.DMA((6,)),
         ],
         compiler_params=pltpu.CompilerParams(collective_id=0, has_side_effects=True, vmem_limit_bytes=58 * 2 ** 20),
         cost_estimate=pl.CostEstimate(flops=7 * 10 ** 9, bytes_accessed=10 ** 7, transcendentals=10 ** 7),
-    )(jnp.transpose(levels_in, (1, 2, 0, 3)), surface, latents, level_codes, norm_gains, regions, *[named[w] for w in WEIGHTS],
-      *[jnp.asarray(m, BF16) for m in permutations()])
+    )(latents, level_codes, norm_gains, regions, *[named[w] for w in WEIGHTS], *loaded)
     return jnp.transpose(decoded, (2, 0, 1, 3))
 
 

time: 90.1 us -> 79.3 us (0.88)
  Pallas kernels: 87.5 us -> 76.7 us
    pallas_call x1, Pallas kernels: 87.5 us -> 76.7 us  [body(): pl.pallas_call(functools.partial(kernel, PLAN), out_shape=jax.ShapeDtypeS...]
where the time goes in v3:
time: 79.3 us; the launch traced here: 79.1 us
  Pallas kernels  76.7 us (97%)
  local copies, waits for them, and re-layouts  2.42 us (3%)
    pallas_call x1, Pallas kernels, body(): pl.pallas_call(functools.partial(kernel, PLAN), out_shape=jax.ShapeDtypeS...  76.7 us
    unnamed x1, local copies, waits for them, and re-layouts  2.42 us

profile of v3, /device:TPU:1, one launch (start us, length us, event | category | flops | bytes accessed | tf_op | source)
XLA Modules:
  0.0 79.1 jit_solution(11545531514519998947)
XLA Ops:
  0.0 76.7 %shard_map.226 = bf16[6,12,13,512]{3,2,1,0:T(8,128)(2,1)} custom-call(bf16[3,512]{1,0:T(4,128)(2,1)} %refs_0_.1, bf16[13,512]{1,0:T(8,128)(2,1)} %refs_1_.1, f32[6,512]{1,0:T(8,128)} %refs_2_.1, s32[4,6]{1,0:T(4,128)} %refs_3_.1, bf16[32,512]{1,0:T(8,128)(2,1)} %refs_4_.1, bf16[32,512]{1,0:T(8,128)(2,1)} %refs_5_.1, bf16[32,512]{1,0:T(8,128)(2,1)} %refs_6_.1, ...), custom_call_target="tpu_custom_call" | custom-call | flops 7000000000 | bytes 10000000 | tf_op jit(solution)/shard_map/pallas_call | solution.py:546
  76.7 2.4 %copy.26 = bf16[13,6,12,512]{3,0,2,1:T(8,128)(2,1)} copy(bf16[13,6,12,512]{3,0,2,1:T(8,128)(2,1)} %bitcast.2) | data formatting | bytes 1916928
